TPU v7x, 512 devices: a whole 4x8x8 slice. The times are simulated.
512 devices in a mesh: ctx: 64 (over z, y_hi, core), kvh: 8 (over y_lo, x).
Axes of the slice: x: 4, y: 8 (y_hi: 4, y_lo: 2; y = y_hi * 2 + y_lo), z: 8, core: 2. Of those that a mesh axis runs over, the one named last changes fastest.
Arguments:
- queries: bfloat16 [8192, 7168], P('ctx', 'kvh'), may hold values from -80 to 80
- keys: bfloat16 [8192, 1024], P('ctx', 'kvh'), may hold values from -4 to 4
- values: bfloat16 [8192, 1024], P('ctx', 'kvh'), may hold values from -6 to 6
- doc_ids: int32 [64], replicated, may hold values from 0 to 7, never falling along the last dimension, each value on 1 to 32 neighbouring positions
- query_pos: int32 [64], replicated, may hold values from 0 to 63, as said below
- selection: int32 [64, 64], replicated, may hold values 0 or 1
Outputs:
- attention: bfloat16 [8192, 7168], P(('ctx', 'kvh'))
- log_total: float32 [56, 8192], P('kvh', 'ctx')
Inputs may be any that keep to these rules, and one draw needn't show every extreme that they name: `doc_ids`: never falling; each document covers 1 to 32 whole blocks, one exactly that many. `query_pos`: each block number once.
All inputs are finite; a program needn't handle non-finite values.
Results may differ from a plain program's by a relative error of at most 0.0044.
Values may be sent and summed in bfloat16 or wider, within the bound.
A program may use at most 128 MiB of HBM per device.

v0:
```python
import jax
import jax.numpy as jnp
from jax import lax
from jax.sharding import PartitionSpec as P

HEAD = 128
BLOCK = 128


def local(queries, keys, values, doc_ids, query_pos, selection):
    row_count = queries.shape[0]
    heads_kv = keys.shape[1] // HEAD
    group_size = queries.shape[1] // (heads_kv * HEAD)
    inverse_root = HEAD ** (-0.5)
    position = lax.axis_index("ctx")
    row_index = jnp.arange(row_count, dtype=jnp.int32)
    global_row = position * row_count + row_index
    query_block = query_pos[global_row // BLOCK]
    query_position = query_block * BLOCK + global_row % BLOCK
    query_doc = doc_ids[query_block]
    block_count = doc_ids.shape[0]
    block_iota = jnp.arange(block_count, dtype=jnp.int32)
    block_open = (query_doc[:, None] == doc_ids[None, :]) & (
        (selection[query_block] == 1) | (block_iota[None, :] == query_block[:, None])
    )
    query_heads = queries.reshape(row_count, heads_kv, group_size, HEAD)
    key_piece = lax.all_gather(keys, "ctx", axis=0, tiled=True)
    value_piece = lax.all_gather(values, "ctx", axis=0, tiled=True)
    key_count = key_piece.shape[0]
    piece_blocks = key_count // BLOCK
    wide_open = jnp.broadcast_to(block_open[:, :, None], (row_count, piece_blocks, BLOCK)).reshape(
        row_count, key_count
    )
    key_position = jnp.arange(key_count, dtype=jnp.int32)
    allowed = wide_open & (key_position[None, :] <= query_position[:, None])
    running_max = jnp.full((row_count, heads_kv, group_size), -1e30, jnp.float32)
    key_heads = key_piece.reshape(key_count, heads_kv, HEAD)
    value_heads = value_piece.reshape(key_count, heads_kv, HEAD)
    scores = (
        jnp.einsum("qhgd,khd->qhgk", query_heads, key_heads, preferred_element_type=jnp.float32)
        * inverse_root
    )
    wide_mask = allowed[:, None, None, :]
    masked = jnp.where(wide_mask, scores, jnp.float32(-1e30))
    new_max = jnp.maximum(running_max, jnp.max(masked, axis=-1))
    weights = jnp.where(wide_mask, jnp.exp(scores - new_max[..., None]), jnp.float32(0.0))
    running_sum = jnp.sum(weights, axis=-1)
    product = jnp.einsum(
        "qhgk,khd->qhgd",
        weights.astype(jnp.bfloat16),
        value_heads,
        preferred_element_type=jnp.float32,
    )
    accumulator = product
    running_max, running_sum, accumulator = (new_max, running_sum, accumulator)
    blended = (
        (accumulator / running_sum[..., None])
        .reshape(row_count, heads_kv * group_size * HEAD)
        .astype(jnp.bfloat16)
    )
    log_rows = (running_max + jnp.log(running_sum)).reshape(row_count, heads_kv * group_size)
    attention = lax.all_to_all(blended, "kvh", split_axis=0, concat_axis=1, tiled=True)
    return (attention, jnp.transpose(log_rows))


def solution(mesh):
    in_specs = (P("ctx", "kvh"), P("ctx", "kvh"), P("ctx", "kvh"), P(), P(), P())
    out_specs = (P(("ctx", "kvh"), None), P("kvh", "ctx"))
    return jax.shard_map(local, mesh=mesh, in_specs=in_specs, out_specs=out_specs, check_vma=False)
```

profile of v0, /device:TPU:1, one launch (start us, length us, event | category | flops | bytes accessed | tf_op | source)
XLA Modules:
  0.0 222.4 jit_solution(17388663615723919254)
XLA Ops:
  7.2 0.0 copy-start
  7.2 0.0 all-gather.3.cloned.1.call-start
  7.2 0.7 all-gather.3.cloned.1.call-update
  7.9 0.0 all-gather.5.cloned.1.call-start
  8.0 0.7 all-gather.5.cloned.1.call-update
  8.7 1.6 gather_fusion
  10.3 0.0 copy-done
  10.3 0.6 gather_fusion.2
  11.0 0.1 copy.22
  11.0 1.6 gather_fusion.1
  12.6 1.1 copy.23
  13.8 0.7 fusion.34
  14.5 0.8 fusion.9
  15.4 86.1 %all-gather.3.cloned.1.call-done = bf16[8192,128]{1,0:T(8,128)(2,1)} async-done(((bf16[128,128]{1,0:T(8,128)(2,1)}), bf16[8192,128]{1,0:T(8,128)(2,1)}) %all-gather.3.cloned.1.call-update) | async-done | bytes 2097168 | tf_op jit(solution)/shard_map/all_gather | solution.py:27
  101.5 13.1 %fusion = (f32[128,7]{0,1:T(8,128)S(1)}, f32[8192,128,7]{1,0,2:T(8,128)}) fusion(pred[128,8192]{0,1:T(8,128)(4,1)S(1)} %fusion.9, bf16[128,7,128]{0,2,1:T(8,128)(2,1)S(1)} %bitcast.83, bf16[8192,128]{1,0:T(8,128)(2,1)} %all-gather.3.cloned.1.call-done), kind=kOutput, calls=%fused_computation.5 | convolution fusion | flops 1901067392 | bytes 32738816 | tf_op jit(solution)/shard_map/qhgd,khd->qhgk/dot_general | solution.py:40
  114.6 12.7 %fusion.3 = f32[128,7]{0,1:T(8,128)S(1)} fusion(f32[8192,128,7]{1,0,2:T(8,128)} %get-tuple-element.3, f32[128,7]{0,1:T(8,128)S(1)} %broadcast_maximum_fusion, pred[128,8192]{0,1:T(8,128)(4,1)S(1)} %fusion.9), kind=kLoop, calls=%fused_computation.8 | loop fusion | flops 29359232 | bytes 30415872 | tf_op jit(solution)/shard_map/reduce_sum | solution.py:47
  127.3 57.8 %all-gather.5.cloned.1.call-done = bf16[8192,128]{1,0:T(8,128)(2,1)} async-done(((bf16[128,128]{1,0:T(8,128)(2,1)}), bf16[8192,128]{1,0:T(8,128)(2,1)}) %all-gather.5.cloned.1.call-update) | async-done | bytes 2097168 | tf_op jit(solution)/shard_map/all_gather | solution.py:28
  185.1 18.6 %fusion.28 = bf16[128,1,7,128]{3,0,2,1:T(8,128)(2,1)S(1)} fusion(bf16[8192,128]{1,0:T(8,128)(2,1)} %all-gather.5.cloned.1.call-done, f32[8192,128,7]{1,0,2:T(8,128)} %get-tuple-element.3, f32[128,7]{0,1:T(8,128)S(1)} %broadcast_maximum_fusion, pred[128,8192]{0,1:T(8,128)(4,1)S(1)} %fusion.9, f32[128,7]{0,1:T(8,128)S(1)} %fusion.3), kind=kOutput, calls=%fused_computation.21 | convolution fusion | flops 1908637696 | bytes 32742400 | tf_op jit(solution)/shard_map/qhgk,khd->qhgd/dot_general | solution.py:48
  203.7 0.2 copy.26
  203.9 1.0 convert_element_type.16
  204.9 4.0 %all-to-all-start = ((bf16[8,16,896]{2,1,0:T(8,128)(2,1)}), bf16[8,16,896]{2,1,0:T(8,128)(2,1)S(1)}, u32[]{:S(2)}, u32[]{:S(2)}) async-start(bf16[8,16,896]{2,1,0:T(8,128)(2,1)} %convert_element_type.16), calls=%async_computation | async-start | bytes 458752 | tf_op jit(solution)/shard_map/all_to_all | solution.py:62
  208.9 0.6 add_bitcast_fusion
  209.5 5.4 %all-to-all-done = bf16[8,16,896]{2,1,0:T(8,128)(2,1)S(1)} async-done(((bf16[8,16,896]{2,1,0:T(8,128)(2,1)}), bf16[8,16,896]{2,1,0:T(8,128)(2,1)S(1)}, u32[]{:S(2)}, u32[]{:S(2)}) %all-to-all-start) | async-done | bytes 229408 | tf_op jit(solution)/shard_map/all_to_all | solution.py:62
  214.9 0.7 copy.30
  (6 shorter events, 0.0 us)
Async XLA Ops:
  7.2 3.1 %copy-start = (s32[64,64]{1,0:T(8,128)S(1)}, s32[64,64]{1,0:T(8,128)}, u32[]{:S(2)}) copy-start(s32[64,64]{1,0:T(8,128)} %param.11) | copy-start | bytes 49156
  7.2 94.3 %all-gather.3.cloned.1.call-start = ((), (), s32[]{:S(2)}) async-start(), calls=%async_computation.1 | async-start | bytes 2129920 | tf_op jit(solution)/shard_map/all_gather | solution.py:27
  7.9 177.2 %all-gather.5.cloned.1.call-start = ((), (), s32[]{:S(2)}) async-start(), calls=%async_computation.2 | async-start | bytes 2129920 | tf_op jit(solution)/shard_map/all_gather | solution.py:28
  204.9 10.0 %all-to-all-start = ((bf16[8,16,896]{2,1,0:T(8,128)(2,1)}), bf16[8,16,896]{2,1,0:T(8,128)(2,1)S(1)}, u32[]{:S(2)}, u32[]{:S(2)}) async-start(bf16[8,16,896]{2,1,0:T(8,128)(2,1)} %convert_element_type.16), calls=%async_computation | async-start | bytes 458752 | tf_op jit(solution)/shard_map/all_to_all | solution.py:62
Sparse Core Ops, SparseCore 0:
  11.4 90.0 all-gather.2
  104.8 80.2 all-gather.4
where the time goes:
time: 223 us; the launch traced here: 222 us
  waiting for transfers between devices  151 us (68%)
  matrix products  31.7 us (14%)
  other arithmetic  15 us (7%)
  between operations  14.1 us (6%)
  local copies, waits for them, and re-layouts  6.86 us (3%)
  starting transfers between devices  4.05 us (2%)
    all_gather x1, waiting for transfers between devices, local(): key_piece = lax.all_gather(keys, 'ctx', axis=0, tiled=True)  86.1 us
    all_gather x1, waiting for transfers between devices, local(): value_piece = lax.all_gather(values, 'ctx', axis=0, tiled=True)  57.8 us
    dot_general x1, matrix products, local(): jnp.einsum('qhgk,khd->qhgd', weights.astype(jnp.bfloat16), value_heads, p...  18.6 us
    dot_general x1, matrix products, local(): jnp.einsum('qhgd,khd->qhgk', query_heads, key_heads, preferred_element_ty...  13.1 us
    reduce_sum x1, other arithmetic, local(): running_sum = jnp.sum(weights, axis=-1)  12.7 us
    all_to_all x1, waiting for transfers between devices, local(): lax.all_to_all(blended, 'kvh', split_axis=0, concat_axis=1, tiled=True)  5.44 us
  transfers between devices with their start and end apart: 3, of which 3 were waited for; matrix products, arithmetic and copies ran while one was open for 15% of the time, Pallas kernels for 0%

commit v1 on v0

v1 whole, which is shorter than its diff:
```python
import functools
import math

import jax
import jax.numpy as jnp
from jax import lax
from jax.experimental import pallas as pl
from jax.experimental.pallas import tpu as pltpu
from jax.sharding import PartitionSpec as P

HEAD = 128
BLOCK = 128
Z, Y = 8, 4
NEG = -1e30
PENALTY = 1e30
INV_ROOT = HEAD ** (-0.5)
SCALE2 = INV_ROOT * math.log2(math.e)
MESH = pl.DeviceIdType.MESH
BOTH = slice(None)

CHUNKS = (
    ((0, 0), (-1, 0), (1, 0), (0, 1)),
    ((0, 3), (-2, 0), (2, 0), (0, 2)),
    ((-1, 1), (1, 1), (-1, 3), (1, 3)),
    ((-3, 0), (3, 0), (-1, 2), (1, 2)),
    ((-2, 1), (2, 1), (-3, 1), (3, 1)),
    ((-3, 3), (3, 3), (-2, 3), (2, 3)),
    ((-2, 2), (2, 2), (4, 0), (4, 1)),
    ((4, 3), (-3, 2), (3, 2), (4, 2)),
)


def kernel(
    groups,
    ranks,
    docs,
    query_pos,
    selection,
    q_hbm,
    k_hbm,
    v_hbm,
    out,
    log_out,
    kv,
    q_in,
    v_in,
    q_t,
    m_ref,
    l_ref,
    acc,
    blended,
    in_sem,
    send_sem,
    near_sem,
    ring_sem,
    far_sem,
    sib_sem,
    a2a_send,
    a2a_recv,
    own_sem,
):
    me, head = lax.axis_index("ctx"), lax.axis_index("kvh")
    z, y, core = me // (2 * Y), (me // 2) % Y, me % 2

    def at(dz, dy, c=core):
        return (((z + dz + Z) % Z) * Y + (y + dy) % Y) * 2 + c

    up, down, sibling = at(1, 0), at(-1, 0), at(0, 0, 1 - core)
    y_next, y_last, y_far = at(0, 1), at(0, 3), at(0, 2)

    k_copy = pltpu.make_async_copy(k_hbm, kv.at[0, me], in_sem.at[0])
    v_copy = pltpu.make_async_copy(v_hbm, v_in, in_sem.at[1])
    q_copy = pltpu.make_async_copy(q_hbm, q_in, in_sem.at[2])
    k_copy.start()
    v_copy.start()
    q_copy.start()

    barrier = pltpu.get_barrier_semaphore()
    for peer in (up, down, y_next, y_last, y_far, sibling):
        pl.semaphore_signal(barrier, inc=1, device_id=(peer, head), device_id_type=MESH)
    for step in range(1, ranks):
        other = lax.rem(head + step, ranks)
        pl.semaphore_signal(barrier, inc=1, device_id=(me, other), device_id_type=MESH)
    v_copy.wait()
    kv[1, me] = v_in[...].T
    k_copy.wait()
    pl.semaphore_wait(barrier, 6 + ranks - 1)

    sent = []

    def describe(slot, part, target, recv):
        ref = kv.at[part, slot]
        return pltpu.make_async_remote_copy(
            src_ref=ref,
            dst_ref=ref,
            send_sem=send_sem.at[len(sent)],
            recv_sem=recv,
            device_id=(target, head),
            device_id_type=MESH,
        )

    def send(slot, part, target, recv):
        copy = describe(slot, part, target, recv)
        copy.start()
        sent.append(copy)

    def arrived(slot, part, recv):
        ref = kv.at[part, slot]
        pltpu.make_async_remote_copy(
            src_ref=ref,
            dst_ref=ref,
            send_sem=send_sem.at[0],
            recv_sem=recv,
            device_id=(sibling, head),
            device_id_type=MESH,
        ).wait_recv()

    def share(dz, dy):
        send(at(dz, dy), BOTH, sibling, sib_sem.at[(dz + Z) % Z, dy])

    def ring_send(side, step, dy):
        behind = -(step - 1) if side == 0 else step - 1
        part = side if step == 4 else BOTH
        send(at(behind, dy), part, (up, down)[side], ring_sem.at[side, step - 1, dy])

    def ring_take(step, dy, onward):
        for side in (0, 1):
            behind = -step if side == 0 else step
            part = side if step == 4 else BOTH
            arrived(at(behind, dy), part, ring_sem.at[side, step - 1, dy])
            if onward:
                ring_send(side, step + 1, dy)
            if step < 4:
                share(behind, dy)
        if step == 4:
            share(4, dy)

    def fan(dz):
        index = {-3: 0, 3: 1, 4: 2}[dz]
        send(at(dz, 0), BOTH, y_next, far_sem.at[index, 1])
        send(at(dz, 0), BOTH, y_last, far_sem.at[index, 0])

    def fan_take(dz):
        index = {-3: 0, 3: 1, 4: 2}[dz]
        for where, dy in ((0, 1), (1, 3)):
            arrived(at(dz, dy), BOTH, far_sem.at[index, where])
            share(dz, dy)

    block = query_pos[me]
    doc = docs[block]

    def penalty(slot):
        fine = (docs[slot] == doc) & (selection[block, slot] == 1) & (slot < block)
        return jnp.where(fine, jnp.float32(0.0), jnp.float32(PENALTY))

    def attend(pairs, last=False):
        slots = [at(dz, dy, 0) for dz, dy in pairs]
        pens = [(penalty(s), penalty(s + 1)) for s in slots]
        for dz, dy in pairs:
            arrived(at(dz, dy, 1 - core), BOTH, sib_sem.at[(dz + Z) % Z, dy])

        def one(g, carry):
            q = q_t[g]
            old = m_ref[g]
            top = old
            scores, values = [], []
            for slot, pen in zip(slots, pens):
                keys = kv[0, pl.ds(slot, 2)].reshape(2 * BLOCK, HEAD)
                s = jnp.dot(keys, q, preferred_element_type=jnp.float32)
                for half in (0, 1):
                    part = s[half * BLOCK : (half + 1) * BLOCK]
                    scores.append((part, pen[half]))
                    most = jnp.max(part.reshape(BLOCK // 8, 8, BLOCK), axis=0)
                    top = jnp.maximum(top, most - pen[half])
                    values.append(kv[1, slot + half])
            if last:
                part = jnp.dot(kv[0, block], q, preferred_element_type=jnp.float32)
                key = lax.broadcasted_iota(jnp.int32, (BLOCK, BLOCK), 0)
                query = lax.broadcasted_iota(jnp.int32, (BLOCK, BLOCK), 1)
                part = jnp.where(key <= query, part, jnp.float32(NEG))
                scores.append((part, jnp.float32(0.0)))
                top = jnp.maximum(top, jnp.max(part.reshape(BLOCK // 8, 8, BLOCK), axis=0))
                values.append(kv[1, block])
            new = jnp.max(top, axis=0, keepdims=True)
            keep = jnp.exp2((old - new) * SCALE2)
            total = l_ref[g] * keep
            weights = []
            for part, pen in scores:
                w = jnp.exp2((part - (new + 3.0 * pen)) * SCALE2)
                total = total + jnp.sum(w.reshape(BLOCK // 8, 8, BLOCK), axis=0)
                weights.append(w.astype(jnp.bfloat16))
            product = jnp.dot(
                jnp.concatenate(values, axis=1),
                jnp.concatenate(weights, axis=0),
                preferred_element_type=jnp.float32,
            )
            sums = acc[g] * keep[0:1] + product
            if last:
                whole = jnp.sum(total, axis=0, keepdims=True)
                ready = (sums / whole).T.astype(jnp.bfloat16)
                blended[:, pl.ds(pl.multiple_of(g * HEAD, HEAD), HEAD)] = ready
                log_out[pl.ds(g, 1), :] = new * INV_ROOT + jnp.log(whole)
            else:
                m_ref[g] = jnp.broadcast_to(new, (8, BLOCK))
                l_ref[g] = total
                acc[g] = sums
            return carry

        lax.fori_loop(0, groups, one, 0)

    ring_send(0, 1, 0)
    ring_send(1, 1, 0)
    send(me, BOTH, y_next, near_sem.at[1])
    send(me, BOTH, y_last, near_sem.at[0])
    share(0, 0)

    q_copy.wait()
    for g in range(groups):
        q_t[g] = q_in[:, g * HEAD : (g + 1) * HEAD].T
    m_ref[...] = jnp.full_like(m_ref, NEG)
    l_ref[...] = jnp.zeros_like(l_ref)
    acc[...] = jnp.zeros_like(acc)

    ring_take(1, 0, True)
    arrived(at(0, 1), BOTH, near_sem.at[0])
    send(at(0, 1), 1, y_last, near_sem.at[3])
    arrived(at(0, 3), BOTH, near_sem.at[1])
    send(at(0, 3), 0, y_next, near_sem.at[2])
    for dy in (1, 3):
        ring_send(0, 1, dy)
        ring_send(1, 1, dy)
        share(0, dy)
    ring_take(2, 0, True)
    attend(CHUNKS[0])
    arrived(at(0, 2), 0, near_sem.at[2])
    arrived(at(0, 2), 1, near_sem.at[3])
    ring_send(0, 1, 2)
    ring_send(1, 1, 2)
    share(0, 2)
    ring_take(1, 1, True)
    ring_take(3, 0, True)
    fan(-3)
    fan(3)
    attend(CHUNKS[1])
    ring_take(1, 3, True)
    ring_take(1, 2, True)
    attend(CHUNKS[2])
    ring_take(4, 0, False)
    fan(4)
    fan_take(-3)
    fan_take(3)
    attend(CHUNKS[3])
    ring_take(2, 2, True)
    ring_take(2, 1, False)
    attend(CHUNKS[4])
    ring_take(2, 3, False)
    fan_take(4)
    attend(CHUNKS[5])
    ring_take(3, 2, True)
    attend(CHUNKS[6])
    ring_take(4, 2, False)
    attend(CHUNKS[7], last=True)

    def strip(r):
        return pl.ds(pl.multiple_of(r * (BLOCK // ranks), BLOCK // ranks), BLOCK // ranks)

    width = groups * HEAD
    columns = pl.ds(pl.multiple_of(head * width, HEAD), width)
    moves = []
    for step in range(1, ranks):
        other = lax.rem(head + step, ranks)
        move = pltpu.make_async_remote_copy(
            src_ref=blended.at[strip(other), :],
            dst_ref=out.at[:, columns],
            send_sem=a2a_send.at[step],
            recv_sem=a2a_recv.at[step],
            device_id=(me, other),
            device_id_type=MESH,
        )
        move.start()
        moves.append(move)
    own = pltpu.make_async_copy(blended.at[strip(head), :], out.at[:, columns], own_sem)
    own.start()
    for copy in sent:
        copy.wait_send()
    for step, move in enumerate(moves, 1):
        source = lax.rem(head - step + ranks, ranks)
        there = pl.ds(pl.multiple_of(source * width, HEAD), width)
        pltpu.make_async_remote_copy(
            src_ref=blended.at[strip(head), :],
            dst_ref=out.at[:, there],
            send_sem=a2a_send.at[step],
            recv_sem=a2a_recv.at[step],
            device_id=(me, source),
            device_id_type=MESH,
        ).wait_recv()
        move.wait_send()
    own.wait()


SENDS = 32 + 2 * (4 + 4 + 2 + 2) + 4 + 6


def local(ranks, queries, keys, values, doc_ids, query_pos, selection):
    rows, width = queries.shape
    groups = width // HEAD
    dma = pltpu.SemaphoreType.DMA
    smem = pl.BlockSpec(memory_space=pltpu.SMEM)
    anywhere = pl.BlockSpec(memory_space=pl.ANY)
    return pl.pallas_call(
        functools.partial(kernel, groups, ranks),
        out_shape=(
            jax.ShapeDtypeStruct((rows // ranks, ranks * width), jnp.bfloat16),
            jax.ShapeDtypeStruct((groups, rows), jnp.float32),
        ),
        in_specs=[smem, smem, smem, anywhere, anywhere, anywhere],
        out_specs=(anywhere, pl.BlockSpec(memory_space=pltpu.VMEM)),
        scratch_shapes=[
            pltpu.VMEM((2, Z * Y * 2, BLOCK, HEAD), jnp.bfloat16),
            pltpu.VMEM((rows, width), jnp.bfloat16),
            pltpu.VMEM((BLOCK, HEAD), jnp.bfloat16),
            pltpu.VMEM((groups, HEAD, BLOCK), jnp.bfloat16),
            pltpu.VMEM((groups, 8, BLOCK), jnp.float32),
            pltpu.VMEM((groups, 8, BLOCK), jnp.float32),
            pltpu.VMEM((groups, HEAD, BLOCK), jnp.float32),
            pltpu.VMEM((rows, width), jnp.bfloat16),
            dma((3,)),
            dma((SENDS,)),
            dma((4,)),
            dma((2, 4, Y)),
            dma((3, 2)),
            dma((Z, Y)),
            dma((ranks,)),
            dma((ranks,)),
            dma,
        ],
        compiler_params=pltpu.CompilerParams(
            collective_id=0, has_side_effects=True, vmem_limit_bytes=32 * 1024 * 1024
        ),
        cost_estimate=pl.CostEstimate(
            flops=4 * rows * width * Z * Y * 2 * BLOCK,
            bytes_accessed=4 * rows * width,
            transcendentals=rows * groups * Z * Y * 2 * BLOCK,
        ),
    )(doc_ids, query_pos, selection, queries, keys, values)


def solution(mesh):
    in_specs = (P("ctx", "kvh"), P("ctx", "kvh"), P("ctx", "kvh"), P(), P(), P())
    out_specs = (P(("ctx", "kvh"), None), P("kvh", "ctx"))
    return jax.shard_map(
        functools.partial(local, mesh.shape["kvh"]),
        mesh=mesh,
        in_specs=in_specs,
        out_specs=out_specs,
        check_vma=False,
    )
```

time: 223 us -> 72.5 us (0.33)
  waiting for transfers between devices: 151 us -> 0 us
  Pallas kernels: 0 us -> 65.6 us
  matrix products: 31.7 us -> 0 us
  other arithmetic: 15 us -> 0 us
  between operations: 14.1 us -> 0.65 us
  starting transfers between devices: 4.05 us -> 0 us
    all_gather x2 -> x0, waiting for transfers between devices: 144 us -> none  [the longest x1 86.1 us: local(): key_piece = lax.all_gather(keys, 'ctx', axis=0, tiled=True)]
    pallas_call x0 -> x1, Pallas kernels: none -> 65.6 us  [local(): pl.pallas_call(functools.partial(kernel, groups, ranks), out_shape=(jax.S...]
    dot_general x2 -> x0, matrix products: 31.7 us -> none  [the longest x1 18.6 us: local(): jnp.einsum('qhgk,khd->qhgd', weights.astype(jnp.bfloat16), value_heads, p...]
    reduce_sum x1 -> x0, other arithmetic: 12.7 us -> none  [local(): running_sum = jnp.sum(weights, axis=-1)]
    all_to_all x1 -> x0, waiting for transfers between devices: 5.44 us -> none  [local(): lax.all_to_all(blended, 'kvh', split_axis=0, concat_axis=1, tiled=True)]
    unnamed x3 -> x14, local copies, waits for them, and re-layouts: 1.13 us -> 5.8 us
    all_to_all x1 -> x0, starting transfers between devices: 3.97 us -> none  [local(): lax.all_to_all(blended, 'kvh', split_axis=0, concat_axis=1, tiled=True)]
    gather x4 -> x0, local copies, waits for them, and re-layouts: 3.9 us -> none  [the longest x1 1.6 us: local(): query_doc = doc_ids[query_block]]
  transfers between devices with their start and end apart: 3 -> 0, of which waited for: 3 -> 0; matrix products, arithmetic and copies ran while one was open for 15% -> 0% of each run, Pallas kernels for 0% -> 0%
where the time goes in v1:
time: 72.5 us; the launch traced here: 72.1 us
  Pallas kernels  65.6 us (90%)
  local copies, waits for them, and re-layouts  5.8 us (8%)
    pallas_call x1, Pallas kernels, local(): pl.pallas_call(functools.partial(kernel, groups, ranks), out_shape=(jax.S...  65.6 us
    unnamed x14, local copies, waits for them, and re-layouts  5.8 us

profile of v1, /device:TPU:1, one launch (start us, length us, event | category | flops | bytes accessed | tf_op | source)
XLA Modules:
  0.0 72.1 jit_solution(403269248212598470)
XLA Ops:
  0.6 0.0 copy-start
  0.6 0.9 %copy-done = bf16[128,896]{1,0:T(8,128)(2,1)S(1)} copy-done((bf16[128,896]{1,0:T(8,128)(2,1)S(1)}, bf16[128,896]{1,0:T(8,128)(2,1)}, u32[]{:S(2)}) %copy-start) | copy-done | bytes 229400
  1.6 0.0 copy-start.1
  1.6 0.8 %copy-done.1 = s32[64,64]{1,0:T(8,128)S(1)} copy-done((s32[64,64]{1,0:T(8,128)S(1)}, s32[64,64]{1,0:T(8,128)}, u32[]{:S(2)}) %copy-start.1) | copy-done | bytes 16408
  2.3 0.0 copy-start.2
  2.3 0.8 %copy-done.2 = bf16[128,128]{1,0:T(8,128)(2,1)S(1)} copy-done((bf16[128,128]{1,0:T(8,128)(2,1)S(1)}, bf16[128,128]{1,0:T(8,128)(2,1)}, u32[]{:S(2)}) %copy-start.2) | copy-done | bytes 32792
  3.1 0.0 copy-start.3
  3.1 0.8 %copy-done.3 = bf16[128,128]{1,0:T(8,128)(2,1)S(1)} copy-done((bf16[128,128]{1,0:T(8,128)(2,1)S(1)}, bf16[128,128]{1,0:T(8,128)(2,1)}, u32[]{:S(2)}) %copy-start.3) | copy-done | bytes 32792
  3.8 0.0 copy-start.4
  3.8 0.7 copy-done.4
  4.5 0.0 copy-start.5
  4.5 0.7 copy-done.5
  5.2 65.6 %shard_map.77 = (bf16[16,7168]{1,0:T(8,128)(2,1)S(1)}, f32[7,128]{1,0:T(8,128)S(1)}) custom-call(s32[64]{0:T(128)S(1)} %copy-done.4, s32[64]{0:T(128)S(1)} %copy-done.5, s32[64,64]{1,0:T(8,128)S(1)} %copy-done.1, bf16[128,896]{1,0:T(8,128)(2,1)S(1)} %copy-done, bf16[128,128]{1,0:T(8,128)(2,1)S(1)} %copy-done.2, bf16[128,128]{1,0:T(8,128)(2,1)S(1)} %copy-done.3), custom_call_target="tpu_custom_call" | custom-call | flops 3758096384 | bytes 458752 | tf_op jit(solution)/shard_map/pallas_call | solution.py:310
  70.8 0.7 copy.10
  71.5 0.6 copy.11
Async XLA Ops:
  0.6 0.9 %copy-start = (bf16[128,896]{1,0:T(8,128)(2,1)S(1)}, bf16[128,896]{1,0:T(8,128)(2,1)}, u32[]{:S(2)}) copy-start(bf16[128,896]{1,0:T(8,128)(2,1)} %q_hbm.1) | copy-start | bytes 688132
  1.6 0.8 %copy-start.1 = (s32[64,64]{1,0:T(8,128)S(1)}, s32[64,64]{1,0:T(8,128)}, u32[]{:S(2)}) copy-start(s32[64,64]{1,0:T(8,128)} %selection.1) | copy-start | bytes 49156
  2.3 0.8 %copy-start.2 = (bf16[128,128]{1,0:T(8,128)(2,1)S(1)}, bf16[128,128]{1,0:T(8,128)(2,1)}, u32[]{:S(2)}) copy-start(bf16[128,128]{1,0:T(8,128)(2,1)} %k_hbm.1) | copy-start | bytes 98308
  3.1 0.8 %copy-start.3 = (bf16[128,128]{1,0:T(8,128)(2,1)S(1)}, bf16[128,128]{1,0:T(8,128)(2,1)}, u32[]{:S(2)}) copy-start(bf16[128,128]{1,0:T(8,128)(2,1)} %v_hbm.1) | copy-start | bytes 98308
  3.8 0.7 copy-start.4
  4.5 0.7 copy-start.5

commit v2 on v1

v2 whole, which is shorter than its diff:
```python
import functools
import math

import jax
import jax.numpy as jnp
from jax import lax
from jax.experimental import pallas as pl
from jax.experimental.pallas import tpu as pltpu
from jax.sharding import PartitionSpec as P

HEAD = 128
BLOCK = 128
Z, Y = 8, 4
NEG = -1e30
PENALTY = 1e30
INV_ROOT = HEAD ** (-0.5)
SCALE2 = INV_ROOT * math.log2(math.e)
MESH = pl.DeviceIdType.MESH
BOTH = slice(None)

WAY_NEXT = {1: "z", 2: "z", 3: "z", 4: "z"}
WAY_FAR = {1: "z", 2: "f", 3: "z", 4: "f"}
ORDER = ((1, 0), (0, 1), (0, 3), (2, 0), (1, 1), (0, 2), (1, 3), (3, 0), (2, 1), (1, 2), (2, 3), (4, 0), (2, 2), (3, 1), (3, 3), (3, 2), (4, 1), (4, 3), (4, 2))
LAG = 2
PER_CHUNK = 4


def way(d, dy):
    if d == 0:
        return "f"
    return "z" if dy == 0 else WAY_FAR[d] if dy == 2 else WAY_NEXT[d]


def rows_of(d):
    return (0,) if d == 0 else (4,) if d == 4 else (-d, d)


def program():
    steps, waiting, due = [], [(0, 0)], []
    for place, (d, dy) in enumerate(ORDER):
        steps.append(("take", d, dy))
        waiting += [(dz, dy) for dz in rows_of(d)]
        while len(waiting) >= PER_CHUNK:
            due.append((place + LAG, waiting[:PER_CHUNK]))
            waiting = waiting[PER_CHUNK:]
        while due and due[0][0] <= place and place < len(ORDER) - 1:
            steps.append(("attend", due.pop(0)[1], False))
    due = [pairs for _, pairs in due] + ([waiting] if waiting else [])
    return steps + [("attend", pairs, i == len(due) - 1) for i, pairs in enumerate(due)]


def kernel(
    groups,
    ranks,
    docs_hbm,
    pos_hbm,
    selection_hbm,
    q_hbm,
    k_hbm,
    v_hbm,
    out,
    log_out,
    kv,
    docs,
    query_pos,
    selection,
    q_in,
    v_in,
    scores,
    q_t,
    m_ref,
    l_ref,
    acc,
    blended,
    in_sem,
    send_sem,
    take_sem,
    sib_sem,
    a2a_send,
    a2a_recv,
    own_sem,
):
    me, head = lax.axis_index("ctx"), lax.axis_index("kvh")
    z, y, core = me // (2 * Y), (me // 2) % Y, me % 2

    def at(dz, dy, c=core):
        return (((z + dz + Z) % Z) * Y + (y + dy) % Y) * 2 + c

    up, down, sibling = at(1, 0), at(-1, 0), at(0, 0, 1 - core)
    y_next, y_last, y_far = at(0, 1), at(0, 3), at(0, 2)

    k_copy = pltpu.make_async_copy(k_hbm, kv.at[0, me], in_sem.at[0])
    v_copy = pltpu.make_async_copy(v_hbm, v_in, in_sem.at[1])
    q_copy = pltpu.make_async_copy(q_hbm, q_in, in_sem.at[2])
    scalars = [
        pltpu.make_async_copy(here, there, in_sem.at[3 + i])
        for i, (here, there) in enumerate(((docs_hbm, docs), (pos_hbm, query_pos), (selection_hbm, selection)))
    ]
    for copy in (v_copy, k_copy, *scalars, q_copy):
        copy.start()

    barrier = pltpu.get_barrier_semaphore()
    for peer in (up, down, y_next, y_last, y_far, sibling):
        pl.semaphore_signal(barrier, inc=1, device_id=(peer, head), device_id_type=MESH)
    for step in range(1, ranks):
        other = lax.rem(head + step, ranks)
        pl.semaphore_signal(barrier, inc=1, device_id=(me, other), device_id_type=MESH)
    v_copy.wait()
    kv[1, me] = v_in[...].T
    k_copy.wait()
    pl.semaphore_wait(barrier, 6 + ranks - 1)

    sent = []

    def describe(slot, part, target, recv):
        ref = kv.at[part, slot]
        return pltpu.make_async_remote_copy(
            src_ref=ref,
            dst_ref=ref,
            send_sem=send_sem.at[len(sent)],
            recv_sem=recv,
            device_id=(target, head),
            device_id_type=MESH,
        )

    def send(slot, part, target, recv):
        copy = describe(slot, part, target, recv)
        copy.start()
        sent.append(copy)

    def arrived(slot, part, recv):
        ref = kv.at[part, slot]
        pltpu.make_async_remote_copy(
            src_ref=ref,
            dst_ref=ref,
            send_sem=send_sem.at[0],
            recv_sem=recv,
            device_id=(sibling, head),
            device_id_type=MESH,
        ).wait_recv()

    def share(dz, dy):
        send(at(dz, dy), BOTH, sibling, sib_sem.at[(dz + Z) % Z, dy])

    def onward(d, dy):
        for side in (0, 1):
            if d < 4 and way(d + 1, dy) == "z":
                part = side if d == 3 else BOTH
                send(at(-d if side == 0 else d, dy), part, (up, down)[side], take_sem.at[side, d + 1, dy])
        for side, dz in enumerate(rows_of(d)):
            if dy == 0 and way(d, 1) == "f":
                send(at(dz, 0), BOTH, y_next, take_sem.at[side, d, 3])
                send(at(dz, 0), BOTH, y_last, take_sem.at[side, d, 1])
            if dy == 0 and way(d, 2) == "f":
                send(at(dz, 0), BOTH, y_far, take_sem.at[side, d, 2])
            share(dz, dy)

    def take(d, dy):
        if d == 4 and way(d, dy) == "z":
            for side in (0, 1):
                arrived(at(4, dy), side, take_sem.at[side, 4, dy])
        else:
            for side, dz in enumerate(rows_of(d)):
                arrived(at(dz, dy), BOTH, take_sem.at[side, d, dy])
        onward(d, dy)

    onward(0, 0)
    q_copy.wait()
    for g in range(groups):
        q_t[:, g * HEAD : (g + 1) * HEAD] = q_in[:, g * HEAD : (g + 1) * HEAD].T
    m_ref[...] = jnp.full_like(m_ref, NEG)
    l_ref[...] = jnp.zeros_like(l_ref)
    acc[...] = jnp.zeros_like(acc)
    for copy in scalars:
        copy.wait()
    block = query_pos[me]
    doc = docs[block]

    def strip(r):
        return pl.ds(pl.multiple_of(r * (BLOCK // ranks), BLOCK // ranks), BLOCK // ranks)

    moves = []

    def hand_out(batch, first, width):
        columns = pl.ds(pl.multiple_of(head * (groups * HEAD) + first, HEAD), width)
        for step in range(1, ranks):
            other = lax.rem(head + step, ranks)
            move = pltpu.make_async_remote_copy(
                src_ref=blended.at[strip(other), pl.ds(first, width)],
                dst_ref=out.at[:, columns],
                send_sem=a2a_send.at[batch, step],
                recv_sem=a2a_recv.at[batch, step],
                device_id=(me, other),
                device_id_type=MESH,
            )
            move.start()
            moves.append((move, batch, step, first, width))
        own = pltpu.make_async_copy(
            blended.at[strip(head), pl.ds(first, width)], out.at[:, columns], own_sem.at[batch]
        )
        own.start()
        moves.append((own, batch, 0, first, width))

    def penalty(slot):
        fine = (docs[slot] == doc) & (selection[block, slot] == 1) & (slot < block)
        return jnp.where(fine, jnp.float32(0.0), jnp.float32(PENALTY))

    def attend(pairs, last=False):
        slots = [at(dz, dy, 0) for dz, dy in pairs]
        pens = [(penalty(s), penalty(s + 1)) for s in slots]
        for dz, dy in pairs:
            arrived(at(dz, dy, 1 - core), BOTH, sib_sem.at[(dz + Z) % Z, dy])

        flat = [(slot + half, pen[half]) for slot, pen in zip(slots, pens) for half in (0, 1)]
        units = [(g, min(2, groups - g)) for g in range(0, groups, 2)]
        key = lax.broadcasted_iota(jnp.int32, (BLOCK, BLOCK), 0)
        query = lax.broadcasted_iota(jnp.int32, (BLOCK, BLOCK), 1)

        def lanes(u):
            g, n = units[u]
            return slice(g * HEAD, (g + n) * HEAD)

        def score(u):
            q, wide = q_t[:, lanes(u)], units[u][1] * HEAD
            for i, slot in enumerate(slots):
                keys = kv[0, pl.ds(slot, 2)].reshape(2 * BLOCK, HEAD)
                scores[u % 2, i * 2 * BLOCK : (i + 1) * 2 * BLOCK, :wide] = jnp.dot(
                    keys, q, preferred_element_type=jnp.float32
                )
            if last:
                part = jnp.dot(kv[0, block], q, preferred_element_type=jnp.float32)
                mask = jnp.concatenate([key <= query] * units[u][1], axis=1)
                end = len(flat) * BLOCK
                scores[u % 2, end : end + BLOCK, :wide] = jnp.where(mask, part, jnp.float32(NEG))

        def blend(u):
            wide = units[u][1] * HEAD
            here = lanes(u)
            parts = flat + ([(block, jnp.float32(0.0))] if last else [])
            old = m_ref[:, here]
            top = old
            for i, (_, pen) in enumerate(parts):
                part = scores[u % 2, i * BLOCK : (i + 1) * BLOCK, :wide]
                top = jnp.maximum(top, jnp.max(part.reshape(BLOCK // 8, 8, wide), axis=0) - pen)
            new = jnp.max(top, axis=0, keepdims=True)
            keep = jnp.exp2((old - new) * SCALE2)
            total = l_ref[:, here] * keep
            weights = []
            for i, (_, pen) in enumerate(parts):
                part = scores[u % 2, i * BLOCK : (i + 1) * BLOCK, :wide]
                w = jnp.exp2((part - (new + 3.0 * pen)) * SCALE2)
                total = total + jnp.sum(w.reshape(BLOCK // 8, 8, wide), axis=0)
                weights.append(w.astype(jnp.bfloat16))
            product = jnp.dot(
                jnp.concatenate([kv[1, slot] for slot, _ in parts], axis=1),
                jnp.concatenate(weights, axis=0),
                preferred_element_type=jnp.float32,
            )
            sums = acc[:, here] * keep[0:1] + product
            if not last:
                m_ref[:, here] = jnp.broadcast_to(new, (8, wide))
                l_ref[:, here] = total
                acc[:, here] = sums
                return
            whole = jnp.sum(total, axis=0, keepdims=True)
            ready = sums / whole
            logs = new * INV_ROOT + jnp.log(whole)
            for j in range(units[u][1]):
                g = units[u][0] + j
                blended[:, g * HEAD : (g + 1) * HEAD] = ready[:, j * HEAD : (j + 1) * HEAD].T.astype(jnp.bfloat16)
                log_out[g : g + 1, :] = logs[:, j * HEAD : (j + 1) * HEAD]

        score(0)
        sent_heads = 0
        for u in range(len(units)):
            if u < len(units) - 1:
                score(u + 1)
            blend(u)
            if last and (u % 2 == 1 or u == len(units) - 1):
                done = sum(units[u])
                hand_out(u // 2, sent_heads * HEAD, (done - sent_heads) * HEAD)
                sent_heads = done

    for kind, *what in program():
        if kind == "take":
            take(*what)
        else:
            attend(*what)

    for copy in sent:
        copy.wait_send()
    for move, batch, step, first, width in moves:
        if step == 0:
            move.wait()
            continue
        source = lax.rem(head - step + ranks, ranks)
        there = pl.ds(pl.multiple_of(source * (groups * HEAD) + first, HEAD), width)
        pltpu.make_async_remote_copy(
            src_ref=blended.at[strip(head), pl.ds(first, width)],
            dst_ref=out.at[:, there],
            send_sem=a2a_send.at[batch, step],
            recv_sem=a2a_recv.at[batch, step],
            device_id=(me, source),
            device_id_type=MESH,
        ).wait_recv()
        move.wait_send()


SENDS = 80


def local(ranks, queries, keys, values, doc_ids, query_pos, selection):
    rows, width = queries.shape
    groups = width // HEAD
    dma = pltpu.SemaphoreType.DMA
    hbm = pl.BlockSpec(memory_space=pltpu.HBM)
    return pl.pallas_call(
        functools.partial(kernel, groups, ranks),
        out_shape=(
            jax.ShapeDtypeStruct((rows // ranks, ranks * width), jnp.bfloat16),
            jax.ShapeDtypeStruct((groups, rows), jnp.float32),
        ),
        in_specs=[hbm] * 6,
        out_specs=(hbm, pl.BlockSpec(memory_space=pltpu.VMEM)),
        scratch_shapes=[
            pltpu.VMEM((2, Z * Y * 2, BLOCK, HEAD), jnp.bfloat16),
            pltpu.SMEM(doc_ids.shape, jnp.int32),
            pltpu.SMEM(query_pos.shape, jnp.int32),
            pltpu.SMEM(selection.shape, jnp.int32),
            pltpu.VMEM((rows, width), jnp.bfloat16),
            pltpu.VMEM((BLOCK, HEAD), jnp.bfloat16),
            pltpu.VMEM((2, (2 * PER_CHUNK + 1) * BLOCK, 2 * BLOCK), jnp.float32),
            pltpu.VMEM((HEAD, width), jnp.bfloat16),
            pltpu.VMEM((8, width), jnp.float32),
            pltpu.VMEM((8, width), jnp.float32),
            pltpu.VMEM((HEAD, width), jnp.float32),
            pltpu.VMEM((rows, width), jnp.bfloat16),
            dma((6,)),
            dma((SENDS,)),
            dma((2, 5, Y)),
            dma((Z, Y)),
            dma((2, ranks)),
            dma((2, ranks)),
            dma((2,)),
        ],
        compiler_params=pltpu.CompilerParams(
            collective_id=0, has_side_effects=True, vmem_limit_bytes=62 * 1024 * 1024
        ),
        cost_estimate=pl.CostEstimate(
            flops=4 * rows * width * Z * Y * 2 * BLOCK,
            bytes_accessed=4 * rows * width,
            transcendentals=rows * groups * Z * Y * 2 * BLOCK,
        ),
    )(doc_ids, query_pos, selection, queries, keys, values)


def solution(mesh):
    in_specs = (P("ctx", "kvh"), P("ctx", "kvh"), P("ctx", "kvh"), P(), P(), P())
    out_specs = (P(("ctx", "kvh"), None), P("kvh", "ctx"))
    return jax.shard_map(
        functools.partial(local, mesh.shape["kvh"]),
        mesh=mesh,
        in_specs=in_specs,
        out_specs=out_specs,
        check_vma=False,
    )
```

time: 72.5 us -> 53.7 us (0.74)
  Pallas kernels: 65.6 us -> 50.7 us
  local copies, waits for them, and re-layouts: 5.8 us -> 2.24 us
    pallas_call x1, Pallas kernels: 65.6 us -> 50.7 us  [local(): pl.pallas_call(functools.partial(kernel, groups, ranks), out_shape=(jax.S...]
    unnamed x14 -> x4, local copies, waits for them, and re-layouts: 5.8 us -> 2.24 us
where the time goes in v2:
time: 53.7 us; the launch traced here: 53.6 us
  Pallas kernels  50.7 us (94%)
  local copies, waits for them, and re-layouts  2.24 us (4%)
  between operations  0.65 us (1%)
    pallas_call x1, Pallas kernels, local(): pl.pallas_call(functools.partial(kernel, groups, ranks), out_shape=(jax.S...  50.7 us
    unnamed x4, local copies, waits for them, and re-layouts  2.24 us

profile of v2, /device:TPU:1, one launch (start us, length us, event | category | flops | bytes accessed | tf_op | source)
XLA Modules:
  0.0 53.6 jit_solution(1090996350031772561)
XLA Ops:
  0.6 50.7 %shard_map.77 = (bf16[16,7168]{1,0:T(8,128)(2,1)}, f32[7,128]{1,0:T(8,128)}) custom-call(s32[64]{0:T(128)} %docs_hbm.1, s32[64]{0:T(128)} %pos_hbm.1, s32[64,64]{1,0:T(8,128)} %selection_hbm.1, bf16[128,896]{1,0:T(8,128)(2,1)} %q_hbm.1, bf16[128,128]{1,0:T(8,128)(2,1)} %k_hbm.1, bf16[128,128]{1,0:T(8,128)(2,1)} %v_hbm.1), custom_call_target="tpu_custom_call" | custom-call | flops 3758096384 | bytes 458752 | tf_op jit(solution)/shard_map/pallas_call | solution.py:317
  51.3 0.0 copy-start
  51.3 1.6 %copy.10 = bf16[16,7168]{1,0:T(8,128)(2,1)} copy(bf16[16,7168]{1,0:T(8,128)(2,1)} %get-tuple-element.4) | data formatting | bytes 458752
  53.0 0.0 copy-done
  53.0 0.6 %copy.11 = f32[7,128]{1,0:T(8,128)} copy(f32[7,128]{1,0:T(8,128)S(1)} %copy-done) | data formatting | bytes 7168
Async XLA Ops:
  51.3 1.7 %copy-start = (f32[7,128]{1,0:T(8,128)S(1)}, f32[7,128]{1,0:T(8,128)}, u32[]{:S(2)}) copy-start(f32[7,128]{1,0:T(8,128)} %get-tuple-element.5) | copy-start | bytes 10756

commit v3 on v2

--- a/solution.py
+++ b/solution.py
@@ -22,7 +22,13 @@
 WAY_FAR = {1: "z", 2: "f", 3: "z", 4: "f"}
 ORDER = ((1, 0), (0, 1), (0, 3), (2, 0), (1, 1), (0, 2), (1, 3), (3, 0), (2, 1), (1, 2), (2, 3), (4, 0), (2, 2), (3, 1), (3, 3), (3, 2), (4, 1), (4, 3), (4, 2))
 LAG = 2
-PER_CHUNK = 4
+PER_BATCH = 2
+BATCHES = 2
+SIZES = (4, 4, 4, 4, 4, 4, 4, 2, 2)
+PER_CHUNK = max(SIZES)
+
+
+PARTS = (0, 1)
 
 
 def way(d, dy):
@@ -36,16 +42,19 @@
 
 
 def program():
-    steps, waiting, due = [], [(0, 0)], []
+    steps, waiting, due, sizes = [], [(0, 0)], [], list(SIZES)
     for place, (d, dy) in enumerate(ORDER):
-        steps.append(("take", d, dy))
+        over = d == 4 and way(d, dy) == "z"
+        for part in PARTS if not over else (0,):
+            for side in (0,) if d == 0 or (d == 4 and not over) else (0, 1):
+                steps.append(("take", side, d, dy, (0, 1)[side] if over else part))
         waiting += [(dz, dy) for dz in rows_of(d)]
-        while len(waiting) >= PER_CHUNK:
-            due.append((place + LAG, waiting[:PER_CHUNK]))
-            waiting = waiting[PER_CHUNK:]
+        while sizes and len(waiting) >= sizes[0]:
+            due.append((place + LAG, waiting[: sizes[0]]))
+            waiting = waiting[sizes.pop(0) :]
         while due and due[0][0] <= place and place < len(ORDER) - 1:
             steps.append(("attend", due.pop(0)[1], False))
-    due = [pairs for _, pairs in due] + ([waiting] if waiting else [])
+    due = [pairs for _, pairs in due]
     return steps + [("attend", pairs, i == len(due) - 1) for i, pairs in enumerate(due)]
 
 
@@ -79,6 +88,8 @@
     a2a_send,
     a2a_recv,
     own_sem,
+    log_in,
+    log_sem,
 ):
     me, head = lax.axis_index("ctx"), lax.axis_index("kvh")
     z, y, core = me // (2 * Y), (me // 2) % Y, me % 2
@@ -105,17 +116,14 @@
     for step in range(1, ranks):
         other = lax.rem(head + step, ranks)
         pl.semaphore_signal(barrier, inc=1, device_id=(me, other), device_id_type=MESH)
-    v_copy.wait()
-    kv[1, me] = v_in[...].T
-    k_copy.wait()
     pl.semaphore_wait(barrier, 6 + ranks - 1)
 
     sent = []
 
-    def describe(slot, part, target, recv):
+    def describe(slot, part, target, recv, origin):
         ref = kv.at[part, slot]
         return pltpu.make_async_remote_copy(
-            src_ref=ref,
+            src_ref=ref if origin is None else origin,
             dst_ref=ref,
             send_sem=send_sem.at[len(sent)],
             recv_sem=recv,
@@ -123,8 +131,8 @@
             device_id_type=MESH,
         )
 
-    def send(slot, part, target, recv):
-        copy = describe(slot, part, target, recv)
+    def send(slot, part, target, recv, origin=None):
+        copy = describe(slot, part, target, recv, origin)
         copy.start()
         sent.append(copy)
 
@@ -142,29 +150,43 @@
     def share(dz, dy):
         send(at(dz, dy), BOTH, sibling, sib_sem.at[(dz + Z) % Z, dy])
 
-    def onward(d, dy):
-        for side in (0, 1):
-            if d < 4 and way(d + 1, dy) == "z":
-                part = side if d == 3 else BOTH
-                send(at(-d if side == 0 else d, dy), part, (up, down)[side], take_sem.at[side, d + 1, dy])
-        for side, dz in enumerate(rows_of(d)):
-            if dy == 0 and way(d, 1) == "f":
-                send(at(dz, 0), BOTH, y_next, take_sem.at[side, d, 3])
-                send(at(dz, 0), BOTH, y_last, take_sem.at[side, d, 1])
-            if dy == 0 and way(d, 2) == "f":
-                send(at(dz, 0), BOTH, y_far, take_sem.at[side, d, 2])
+    def onward(side, d, dy, part):
+        origin = k_hbm if (d, dy, part) == (0, 0, 0) else None
+        dz = 0 if d == 0 else -d if side == 0 else d
+        index = PARTS.index(part)
+        if d < 4 and way(d + 1, dy) == "z":
+            for s in (0, 1) if d == 0 else (side,):
+                piece = part
+                if d == 3:
+                    if part != BOTH and part != s:
+                        continue
+                    piece = s
+                    index = 0
+                send(at(dz, dy), piece, (up, down)[s], take_sem.at[s, d + 1, dy, index], origin)
+        index = PARTS.index(part)
+        if dy == 0 and way(d, 1) == "f":
+            send(at(dz, 0), part, y_next, take_sem.at[side, d, 3, index], origin)
+            send(at(dz, 0), part, y_last, take_sem.at[side, d, 1, index], origin)
+        if dy == 0 and way(d, 2) == "f":
+            send(at(dz, 0), part, y_far, take_sem.at[side, d, 2, index], origin)
+        if part == PARTS[-1]:
             share(dz, dy)
 
-    def take(d, dy):
-        if d == 4 and way(d, dy) == "z":
-            for side in (0, 1):
-                arrived(at(4, dy), side, take_sem.at[side, 4, dy])
-        else:
-            for side, dz in enumerate(rows_of(d)):
-                arrived(at(dz, dy), BOTH, take_sem.at[side, d, dy])
-        onward(d, dy)
-
-    onward(0, 0)
+    def take(side, d, dy, part):
+        over = d == 4 and way(d, dy) == "z"
+        dz = 0 if d == 0 else -d if side == 0 else d
+        arrived(at(dz, dy), part, take_sem.at[side, d, dy, 0 if over else PARTS.index(part)])
+        if not over:
+            onward(side, d, dy, part)
+        elif side == 1:
+            for piece in PARTS:
+                onward(0, d, dy, piece)
+
+    onward(0, 0, 0, 0)
+    v_copy.wait()
+    kv[1, me] = v_in[...].T
+    k_copy.wait()
+    onward(0, 0, 0, 1)
     q_copy.wait()
     for g in range(groups):
         q_t[:, g * HEAD : (g + 1) * HEAD] = q_in[:, g * HEAD : (g + 1) * HEAD].T
@@ -182,12 +204,12 @@
     moves = []
 
     def hand_out(batch, first, width):
-        columns = pl.ds(pl.multiple_of(head * (groups * HEAD) + first, HEAD), width)
+        columns = pl.ds(first, width)
         for step in range(1, ranks):
             other = lax.rem(head + step, ranks)
             move = pltpu.make_async_remote_copy(
                 src_ref=blended.at[strip(other), pl.ds(first, width)],
-                dst_ref=out.at[:, columns],
+                dst_ref=out.at[head, :, columns],
                 send_sem=a2a_send.at[batch, step],
                 recv_sem=a2a_recv.at[batch, step],
                 device_id=(me, other),
@@ -196,7 +218,7 @@
             move.start()
             moves.append((move, batch, step, first, width))
         own = pltpu.make_async_copy(
-            blended.at[strip(head), pl.ds(first, width)], out.at[:, columns], own_sem.at[batch]
+            blended.at[strip(head), pl.ds(first, width)], out.at[head, :, columns], own_sem.at[batch]
         )
         own.start()
         moves.append((own, batch, 0, first, width))
@@ -268,7 +290,7 @@
             for j in range(units[u][1]):
                 g = units[u][0] + j
                 blended[:, g * HEAD : (g + 1) * HEAD] = ready[:, j * HEAD : (j + 1) * HEAD].T.astype(jnp.bfloat16)
-                log_out[g : g + 1, :] = logs[:, j * HEAD : (j + 1) * HEAD]
+                log_in[g : g + 1, :] = logs[:, j * HEAD : (j + 1) * HEAD]
 
         score(0)
         sent_heads = 0
@@ -276,10 +298,12 @@
             if u < len(units) - 1:
                 score(u + 1)
             blend(u)
-            if last and (u % 2 == 1 or u == len(units) - 1):
+            if last and (u % PER_BATCH == PER_BATCH - 1 or u == len(units) - 1):
                 done = sum(units[u])
-                hand_out(u // 2, sent_heads * HEAD, (done - sent_heads) * HEAD)
+                hand_out(u // PER_BATCH, sent_heads * HEAD, (done - sent_heads) * HEAD)
                 sent_heads = done
+        if last:
+            pltpu.make_async_copy(log_in, log_out, log_sem).start()
 
     for kind, *what in program():
         if kind == "take":
@@ -294,19 +318,19 @@
             move.wait()
             continue
         source = lax.rem(head - step + ranks, ranks)
-        there = pl.ds(pl.multiple_of(source * (groups * HEAD) + first, HEAD), width)
         pltpu.make_async_remote_copy(
             src_ref=blended.at[strip(head), pl.ds(first, width)],
-            dst_ref=out.at[:, there],
+            dst_ref=out.at[source, :, pl.ds(first, width)],
             send_sem=a2a_send.at[batch, step],
             recv_sem=a2a_recv.at[batch, step],
             device_id=(me, source),
             device_id_type=MESH,
         ).wait_recv()
         move.wait_send()
-
-
-SENDS = 80
+    pltpu.make_async_copy(log_in, log_out, log_sem).wait()
+
+
+SENDS = 160
 
 
 def local(ranks, queries, keys, values, doc_ids, query_pos, selection):
@@ -314,14 +338,14 @@
     groups = width // HEAD
     dma = pltpu.SemaphoreType.DMA
     hbm = pl.BlockSpec(memory_space=pltpu.HBM)
-    return pl.pallas_call(
+    strips, logs = pl.pallas_call(
         functools.partial(kernel, groups, ranks),
         out_shape=(
-            jax.ShapeDtypeStruct((rows // ranks, ranks * width), jnp.bfloat16),
+            jax.ShapeDtypeStruct((ranks, rows // ranks, width), jnp.bfloat16),
             jax.ShapeDtypeStruct((groups, rows), jnp.float32),
         ),
         in_specs=[hbm] * 6,
-        out_specs=(hbm, pl.BlockSpec(memory_space=pltpu.VMEM)),
+        out_specs=(hbm, hbm),
         scratch_shapes=[
             pltpu.VMEM((2, Z * Y * 2, BLOCK, HEAD), jnp.bfloat16),
             pltpu.SMEM(doc_ids.shape, jnp.int32),
@@ -337,11 +361,13 @@
             pltpu.VMEM((rows, width), jnp.bfloat16),
             dma((6,)),
             dma((SENDS,)),
-            dma((2, 5, Y)),
+            dma((2, 5, Y, 2)),
             dma((Z, Y)),
-            dma((2, ranks)),
-            dma((2, ranks)),
-            dma((2,)),
+            dma((BATCHES, ranks)),
+            dma((BATCHES, ranks)),
+            dma((BATCHES,)),
+            pltpu.VMEM((groups, rows), jnp.float32),
+            dma,
         ],
         compiler_params=pltpu.CompilerParams(
             collective_id=0, has_side_effects=True, vmem_limit_bytes=62 * 1024 * 1024
@@ -352,6 +378,7 @@
             transcendentals=rows * groups * Z * Y * 2 * BLOCK,
         ),
     )(doc_ids, query_pos, selection, queries, keys, values)
+    return jnp.transpose(strips, (1, 0, 2)).reshape(rows // ranks, ranks * width), logs
 
 
 def solution(mesh):

time: 53.7 us -> 52.7 us (0.981)
  Pallas kernels: 50.7 us -> 49.6 us
    reshape x0 -> x1, local copies, waits for them, and re-layouts: none -> 1.65 us  [local(): jnp.transpose(strips, (1, 0, 2)).reshape(rows // ranks, ranks * width)]
    unnamed x4 -> x3, local copies, waits for them, and re-layouts: 2.24 us -> 0.6 us
    pallas_call x1, Pallas kernels: 50.7 us -> 49.6 us  [local(): pl.pallas_call(functools.partial(kernel, groups, ranks), out_shape=(jax.S...]
where the time goes in v3:
time: 52.7 us; the launch traced here: 52.5 us
  Pallas kernels  49.6 us (94%)
  local copies, waits for them, and re-layouts  2.24 us (4%)
  between operations  0.65 us (1%)
    pallas_call x1, Pallas kernels, local(): pl.pallas_call(functools.partial(kernel, groups, ranks), out_shape=(jax.S...  49.6 us
    reshape x1, local copies, waits for them, and re-layouts, local(): jnp.transpose(strips, (1, 0, 2)).reshape(rows // ranks, ranks * width)  1.65 us

profile of v3, /device:TPU:1, one launch (start us, length us, event | category | flops | bytes accessed | tf_op | source)
XLA Modules:
  0.0 52.5 jit_solution(8034703381384851766)
XLA Ops:
  0.6 49.6 %shard_map.77 = (bf16[8,16,896]{2,1,0:T(8,128)(2,1)}, f32[7,128]{1,0:T(8,128)}) custom-call(s32[64]{0:T(128)} %docs_hbm.1, s32[64]{0:T(128)} %pos_hbm.1, s32[64,64]{1,0:T(8,128)} %selection_hbm.1, bf16[128,896]{1,0:T(8,128)(2,1)} %q_hbm.1, bf16[128,128]{1,0:T(8,128)(2,1)} %k_hbm.1, bf16[128,128]{1,0:T(8,128)(2,1)} %v_hbm.1), custom_call_target="tpu_custom_call" | custom-call | flops 3758096384 | bytes 458752 | tf_op jit(solution)/shard_map/pallas_call | solution.py:341
  50.3 0.0 copy-start
  50.3 1.6 %copy.9 = bf16[8,2,8,896]{3,2,0,1:T(8,128)(2,1)} copy(bf16[8,2,8,896]{3,2,1,0:T(8,128)(2,1)} %bitcast.4) | data formatting | bytes 458752 | tf_op jit(solution)/shard_map/reshape | solution.py:381
  51.9 0.0 copy-done
  51.9 0.6 %copy.11 = f32[7,128]{1,0:T(8,128)} copy(f32[7,128]{1,0:T(8,128)S(1)} %copy-done) | data formatting | bytes 7168
Async XLA Ops:
  50.3 1.7 %copy-start = (f32[7,128]{1,0:T(8,128)S(1)}, f32[7,128]{1,0:T(8,128)}, u32[]{:S(2)}) copy-start(f32[7,128]{1,0:T(8,128)} %get-tuple-element.9) | copy-start | bytes 10756

commit v4 on v3

--- a/solution.py
+++ b/solution.py
@@ -20,7 +20,7 @@
 
 WAY_NEXT = {1: "z", 2: "z", 3: "z", 4: "z"}
 WAY_FAR = {1: "z", 2: "f", 3: "z", 4: "f"}
-ORDER = ((1, 0), (0, 1), (0, 3), (2, 0), (1, 1), (0, 2), (1, 3), (3, 0), (2, 1), (1, 2), (2, 3), (4, 0), (2, 2), (3, 1), (3, 3), (3, 2), (4, 1), (4, 3), (4, 2))
+ORDER = ((1, 0), (0, 1), (0, 3), (2, 0), (1, 1), (0, 2), (1, 3), (3, 0), (2, 1), (2, 3), (1, 2), (4, 0), (2, 2), (3, 1), (3, 3), (4, 1), (4, 3), (3, 2), (4, 2))
 LAG = 2
 PER_BATCH = 2
 BATCHES = 2
@@ -107,8 +107,8 @@
         pltpu.make_async_copy(here, there, in_sem.at[3 + i])
         for i, (here, there) in enumerate(((docs_hbm, docs), (pos_hbm, query_pos), (selection_hbm, selection)))
     ]
-    for copy in (v_copy, k_copy, *scalars, q_copy):
-        copy.start()
+    v_copy.start()
+    k_copy.start()
 
     barrier = pltpu.get_barrier_semaphore()
     for peer in (up, down, y_next, y_last, y_far, sibling):
@@ -116,6 +116,8 @@
     for step in range(1, ranks):
         other = lax.rem(head + step, ranks)
         pl.semaphore_signal(barrier, inc=1, device_id=(me, other), device_id_type=MESH)
+    for copy in (*scalars, q_copy):
+        copy.start()
     pl.semaphore_wait(barrier, 6 + ranks - 1)
 
     sent = []

time: 52.7 us -> 53.8 us (1.021)
  Pallas kernels: 49.6 us -> 50.8 us
    pallas_call x1, Pallas kernels: 49.6 us -> 50.8 us  [local(): pl.pallas_call(functools.partial(kernel, groups, ranks), out_shape=(jax.S...]
where the time goes in v4:
time: 53.8 us; the launch traced here: 53.6 us
  Pallas kernels  50.8 us (94%)
  local copies, waits for them, and re-layouts  2.24 us (4%)
  between operations  0.65 us (1%)
    pallas_call x1, Pallas kernels, local(): pl.pallas_call(functools.partial(kernel, groups, ranks), out_shape=(jax.S...  50.8 us
    reshape x1, local copies, waits for them, and re-layouts, local(): jnp.transpose(strips, (1, 0, 2)).reshape(rows // ranks, ranks * width)  1.65 us

profile of v4, /device:TPU:1, one launch (start us, length us, event | category | flops | bytes accessed | tf_op | source)
XLA Modules:
  0.0 53.6 jit_solution(11225908352014722515)
XLA Ops:
  0.6 50.8 %shard_map.77 = (bf16[8,16,896]{2,1,0:T(8,128)(2,1)}, f32[7,128]{1,0:T(8,128)}) custom-call(s32[64]{0:T(128)} %docs_hbm.1, s32[64]{0:T(128)} %pos_hbm.1, s32[64,64]{1,0:T(8,128)} %selection_hbm.1, bf16[128,896]{1,0:T(8,128)(2,1)} %q_hbm.1, bf16[128,128]{1,0:T(8,128)(2,1)} %k_hbm.1, bf16[128,128]{1,0:T(8,128)(2,1)} %v_hbm.1), custom_call_target="tpu_custom_call" | custom-call | flops 3758096384 | bytes 458752 | tf_op jit(solution)/shard_map/pallas_call | solution.py:343
  51.4 0.0 copy-start
  51.4 1.6 %copy.9 = bf16[8,2,8,896]{3,2,0,1:T(8,128)(2,1)} copy(bf16[8,2,8,896]{3,2,1,0:T(8,128)(2,1)} %bitcast.4) | data formatting | bytes 458752 | tf_op jit(solution)/shard_map/reshape | solution.py:383
  53.0 0.0 copy-done
  53.0 0.6 %copy.11 = f32[7,128]{1,0:T(8,128)} copy(f32[7,128]{1,0:T(8,128)S(1)} %copy-done) | data formatting | bytes 7168
Async XLA Ops:
  51.4 1.7 %copy-start = (f32[7,128]{1,0:T(8,128)S(1)}, f32[7,128]{1,0:T(8,128)}, u32[]{:S(2)}) copy-start(f32[7,128]{1,0:T(8,128)} %get-tuple-element.9) | copy-start | bytes 10756
